TPU v7x, 512 devices: a whole 4x8x8 slice. The times are simulated.
512 devices in a mesh: row: 32 (over y, x), layer: 16 (over z, core).
Axes of the slice: x: 4, y: 8, z: 8, core: 2. Of those that a mesh axis runs over, the one named last changes fastest.
Arguments:
- panel_left: bfloat16 [32, 32, 2048, 128], P('row', 'layer'), may hold values from -6 to 6
- panel_right: bfloat16 [32, 32, 2048, 128], P('row', 'layer'), may hold values from -0.125 to 0.125
- test_matrix: bfloat16 [2048, 128], replicated, may hold values from -6 to 6
- ranks: int32 [32, 32], P('row', 'layer'), may hold values from 32 to 128, as said below
- offsets: int32 [32, 2], P('row'), may hold values from 1 to 4, as said below
Outputs:
- basis: float32 [32, 2048, 2, 128], P('row', 'layer')
- update_right: float32 [32, 2048, 2, 128], P('row', 'layer')
Inputs may be any that keep to these rules, and one draw needn't show every extreme that they name: `ranks`: some tile has rank 128 and some tile has rank 128 // 4. An owner's 2 offsets differ from each other; the values 1 and 4 occur in every draw.
All inputs are finite; a program needn't handle non-finite values.
Results may differ from a plain program's by a relative error of at most 0.0003.
Values may be sent and summed in bfloat16 or wider, within the bound.
A program may use at most 64 MiB of HBM per device.

v0:
```python
import jax
import jax.numpy as jnp
from jax import lax
from jax.sharding import PartitionSpec as P

FRONTS = 4
TARGETS = 2


def passed_along(x, axis, by):
    length = lax.axis_size(axis)
    return lax.ppermute(x, axis, [(i, (i + by) % length) for i in range(length)])


def constant_of(front_item):
    return lambda: front_item


def orthonormal(sketch_rows, gram_mat):
    factor = jnp.linalg.cholesky(gram_mat)
    by_cols = jnp.transpose(sketch_rows, (1, 2, 0))
    solved = lax.linalg.triangular_solve(factor, by_cols, left_side=True, lower=True)
    return jnp.transpose(solved, (2, 0, 1))


def gram_of(sketch_rows, tile_size):
    return (
        jnp.einsum("bsr,bsq->srq", sketch_rows, sketch_rows, precision=lax.Precision.HIGHEST)
        / tile_size
    )


def on_device(panel_left, panel_right, test_matrix, ranks, offsets):
    high = lax.Precision.HIGHEST
    tile_size = panel_left.shape[2]
    rank_cap = panel_left.shape[3]
    share_rows = tile_size // lax.axis_size("layer")
    columns = lax.broadcasted_iota(jnp.int32, (ranks.shape[1], 1, rank_cap), 2)
    live_cols = (columns < ranks[0][:, None, None]).astype(jnp.bfloat16)
    own_left = panel_left[0] * live_cols
    own_right = panel_right[0] * live_cols
    stacked = jnp.stack([own_left, own_right])
    fronts = []
    moving = stacked
    for step_no in range(FRONTS):
        moving = passed_along(moving, "row", 1)
        fronts.append(moving)
    branches = [constant_of(front_item) for front_item in fronts]
    left_full = own_left.astype(jnp.float32)
    cores = []
    mixers = []
    partners = []
    for target in range(TARGETS):
        partner = lax.switch(offsets[0, target] - 1, branches)
        core_mat = jnp.einsum(
            "kbr,kbq->krq", own_right, partner[1], preferred_element_type=jnp.float32
        )
        probes = jnp.einsum(
            "kbr,bq->krq", partner[0], test_matrix, preferred_element_type=jnp.float32
        )
        mix_mat = jnp.einsum("krq,kqs->krs", core_mat, probes, precision=high)
        cores.append(core_mat)
        mixers.append(mix_mat)
        partners.append(partner[0].astype(jnp.float32))
    mixed = jnp.stack(mixers, axis=1)
    local_sketch = jnp.einsum("kbr,ksrq->bsq", left_full, mixed, precision=high)
    total_sketch = lax.psum(local_sketch, "layer")
    basis_all = orthonormal(total_sketch, gram_of(total_sketch, tile_size))
    first_own = lax.axis_index("layer") * share_rows
    basis_part = lax.dynamic_slice_in_dim(basis_all, first_own, share_rows, 0)
    reach = jnp.einsum("kbr,bsq->ksrq", left_full, basis_all, precision=high)
    weights = []
    for target in range(TARGETS):
        weight_mat = jnp.einsum("krq,krs->kqs", cores[target], reach[:, target], precision=high)
        weights.append(weight_mat)
    term_list = []
    for target in range(TARGETS):
        row_piece = lax.slice_in_dim(
            partners[target], 0, share_rows * lax.axis_size("layer"), axis=1
        )
        term_list.append(jnp.einsum("kbq,kqs->bs", row_piece, weights[target], precision=high))
    update_right = lax.psum_scatter(
        jnp.stack(term_list, axis=1) / tile_size, "layer", scatter_dimension=0, tiled=True
    )
    return (basis_part[None], update_right[None])


def solution(mesh):
    return jax.shard_map(
        on_device,
        mesh=mesh,
        in_specs=(
            P("row", "layer", None, None),
            P("row", "layer", None, None),
            P(),
            P("row", "layer"),
            P("row", None),
        ),
        out_specs=(P("row", "layer", None, None), P("row", "layer", None, None)),
        check_vma=False,
    )
```

profile of v0, /device:TPU:2, one launch (start us, length us, event | category | flops | bytes accessed | tf_op | source)
XLA Modules:
  0.0 479.9 jit_solution(14630520279900826652)
XLA Ops:
  7.2 0.0 copy-start
  7.2 0.0 all-reduce.2.cloned.1.call-start
  7.2 0.8 compare_convert_fusion
  8.0 1.7 broadcast_multiply_fusion.1
  9.7 0.0 copy-start.10
  9.7 0.2 pad_maximum_fusion
  9.9 3.4 collective-permute-start
  13.3 45.9 %collective-permute-done = bf16[2,2,2048,128]{3,2,1,0:T(8,128)(2,1)S(1)} collective-permute-done((bf16[2,2,2048,128]{3,2,1,0:T(8,128)(2,1)S(1)}, bf16[2,2,2048,128]{3,2,1,0:T(8,128)(2,1)S(1)}, u32[]{:S(2)}, u32[]{:S(2)}) %collective-permute-start) | collective-permute-done | bytes 2097184 | tf_op jit(solution)/shard_map/ppermute | solution.py:12
  59.2 3.4 collective-permute-start.1
  62.6 44.0 %collective-permute-done.1 = bf16[2,2,2048,128]{3,2,1,0:T(8,128)(2,1)S(1)} collective-permute-done((bf16[2,2,2048,128]{3,2,1,0:T(8,128)(2,1)S(1)}, bf16[2,2,2048,128]{3,2,1,0:T(8,128)(2,1)S(1)}, u32[]{:S(2)}, u32[]{:S(2)}) %collective-permute-start.1) | collective-permute-done | bytes 2097184 | tf_op jit(solution)/shard_map/ppermute | solution.py:12
  106.6 4.4 collective-permute-start.2
  110.9 43.6 %collective-permute-done.2 = bf16[2,2,2048,128]{3,2,1,0:T(8,128)(2,1)} collective-permute-done((bf16[2,2,2048,128]{3,2,1,0:T(8,128)(2,1)S(1)}, bf16[2,2,2048,128]{3,2,1,0:T(8,128)(2,1)}, u32[]{:S(2)}, u32[]{:S(2)}) %collective-permute-start.2) | collective-permute-done | bytes 2097184 | tf_op jit(solution)/shard_map/ppermute | solution.py:12
  154.5 4.0 collective-permute-start.3
  158.5 0.6 fusion.27
  160.4 41.0 %collective-permute-done.3 = bf16[2,2,2048,128]{3,2,1,0:T(8,128)(2,1)} collective-permute-done((bf16[2,2,2048,128]{3,2,1,0:T(8,128)(2,1)}, bf16[2,2,2048,128]{3,2,1,0:T(8,128)(2,1)}, u32[]{:S(2)}, u32[]{:S(2)}) %collective-permute-start.3) | collective-permute-done | bytes 2097184 | tf_op jit(solution)/shard_map/ppermute | solution.py:12
  201.4 3.1 conditional.2
  201.4 3.1 copy.36
  204.5 2.0 fusion.8
  206.5 2.2 fusion.7
  208.7 0.0 copy-done.8
  208.8 0.5 fusion.11
  209.2 0.1 copy-done.6
  209.4 0.5 fusion.12
  209.9 0.3 convolution_bitcast_fusion.4
  210.1 0.3 convolution_bitcast_fusion.3
  210.4 2.3 convolution_bitcast_fusion
  212.7 0.0 all-reduce.2.cloned.1.call-update
  212.8 0.2 reduce-scatter.2.cloned.1.call-start
  213.0 138.5 %all-reduce.2.cloned.1.call-done = f32[2048,2,128]{2,0,1:T(8,128)} async-done(((f32[2048,2,128]{2,0,1:T(8,128)}), f32[2048,2,128]{2,0,1:T(8,128)}) %all-reduce.2.cloned.1.call-update) | async-done | bytes 2097168 | tf_op jit(solution)/shard_map/psum | solution.py:67
  351.6 5.8 %fusion.28 = f32[2,128,128]{2,1,0:T(8,128)S(1)} fusion(f32[2048,2,128]{2,0,1:T(8,128)} %all-reduce.2.cloned.1.call-done), kind=kOutput, calls=%fused_computation.51 | convolution fusion | flops 805306368 | bytes 2228224 | tf_op jit(solution)/shard_map/bsr,bsq->srq/dot_general | solution.py:28
  357.4 0.1 copy.18
  357.5 23.5 %custom-call.7 = f32[2,128,128]{2,1,0:T(8,128)S(1)} custom-call(f32[2,128,128]{2,1,0:T(8,128)S(1)} %fusion.25), custom_call_target="Cholesky" | custom-call | tf_op jit(solution)/shard_map/jit(cholesky)/cholesky | solution.py:20
  381.0 0.1 compare_reduce_fusion
  381.1 0.1 select_bitcast_fusion
  381.2 19.9 %custom-call.8 = f32[2,1,128,128]{2,3,1,0:T(8,128)S(1)} custom-call(f32[2,1,128,128]{3,2,1,0:T(8,128)S(1)} %select_bitcast_fusion), custom_call_target="InvertDiagBlocksLowerTriangular" | custom-call | tf_op jit(solution)/shard_map/triangular_solve | solution.py:22
  401.2 2.0 fusion.2
  403.1 1.2 fusion.4
  404.3 0.4 fusion.22
  404.7 0.4 fusion.23
  405.1 0.3 copy-done.7
  405.5 1.0 convolution_bitcast_fusion.1
  406.5 1.0 convolution_bitcast_fusion.2
  407.5 1.4 maximum_multiply_fusion
  409.0 0.0 reduce-scatter.2.cloned.1.call-update
  409.0 0.9 dynamic-slice_bitcast_fusion
  409.9 0.8 copy.21
  410.7 60.7 %reduce-scatter.2.cloned.1.call-done = f32[128,2,128]{2,0,1:T(8,128)} async-done(((f32[2048,2,128]{2,0,1:T(8,128)}), f32[128,2,128]{2,0,1:T(8,128)}) %reduce-scatter.2.cloned.1.call-update) | async-done | bytes 131088 | tf_op jit(solution)/shard_map/reduce_scatter | solution.py:82
  471.4 1.7 copy.22
  (22 shorter events, 0.1 us)
Async XLA Ops:
  7.2 201.6 %copy-start = (bf16[2048,128]{1,0:T(8,128)(2,1)S(1)}, bf16[2048,128]{1,0:T(8,128)(2,1)}, u32[]{:S(2)}) copy-start(bf16[2048,128]{1,0:T(8,128)(2,1)} %param.15) | copy-start | bytes 1572868
  7.2 344.4 %all-reduce.2.cloned.1.call-start = ((), (), s32[]{:S(2)}) async-start(), calls=%async_computation.1 | async-start | bytes 4194304 | tf_op jit(solution)/shard_map/psum | solution.py:67
  9.7 148.8 %copy-start.10 = (s32[1,2]{1,0:T(1,128)S(1)}, s32[1,2]{1,0:T(1,128)}, u32[]{:S(2)}) copy-start(s32[1,2]{1,0:T(1,128)} %param.17) | copy-start | bytes 28
  9.9 49.3 %collective-permute-start = (bf16[2,2,2048,128]{3,2,1,0:T(8,128)(2,1)S(1)}, bf16[2,2,2048,128]{3,2,1,0:T(8,128)(2,1)S(1)}, u32[]{:S(2)}, u32[]{:S(2)}) collective-permute-start(bf16[2,2,2048,128]{3,2,1,0:T(8,128)(2,1)S(1)} %pad_maximum_fusion), channel_id=1, source_target_pairs={{0,16},{16,32},{32,48},{48,64},{64,80},{80,96},{96,112},{112,128},... | collective-permute-start | bytes 6291464 | tf_op jit(solution)/shard_map/ppermute | solution.py:12
  59.2 142.2 %copy-start.5 = (bf16[2,2,2048,128]{3,2,1,0:T(8,128)(2,1)}, bf16[2,2,2048,128]{3,2,1,0:T(8,128)(2,1)S(1)}, u32[]{:S(2)}) copy-start(bf16[2,2,2048,128]{3,2,1,0:T(8,128)(2,1)S(1)} %collective-permute-done) | copy-start | bytes 6291460
  59.2 47.4 %collective-permute-start.1 = (bf16[2,2,2048,128]{3,2,1,0:T(8,128)(2,1)S(1)}, bf16[2,2,2048,128]{3,2,1,0:T(8,128)(2,1)S(1)}, u32[]{:S(2)}, u32[]{:S(2)}) collective-permute-start(bf16[2,2,2048,128]{3,2,1,0:T(8,128)(2,1)S(1)} %collective-permute-done), channel_id=1, source_target_pairs={{0,16},{16,32},{32,48},{48,64},{64,80},{80,96},{96,112},{112,128},... | collective-permute-start | bytes 6291464 | tf_op jit(solution)/shard_map/ppermute | solution.py:12
  106.6 48.0 %collective-permute-start.2 = (bf16[2,2,2048,128]{3,2,1,0:T(8,128)(2,1)S(1)}, bf16[2,2,2048,128]{3,2,1,0:T(8,128)(2,1)}, u32[]{:S(2)}, u32[]{:S(2)}) collective-permute-start(bf16[2,2,2048,128]{3,2,1,0:T(8,128)(2,1)S(1)} %collective-permute-done.1), channel_id=1, source_target_pairs={{0,16},{16,32},{32,48},{48,64},{64,80},{80,96},{96,112},{112,128},... | collective-permute-start | bytes 6291464 | tf_op jit(solution)/shard_map/ppermute | solution.py:12
  154.5 46.9 %collective-permute-start.3 = (bf16[2,2,2048,128]{3,2,1,0:T(8,128)(2,1)}, bf16[2,2,2048,128]{3,2,1,0:T(8,128)(2,1)}, u32[]{:S(2)}, u32[]{:S(2)}) collective-permute-start(bf16[2,2,2048,128]{3,2,1,0:T(8,128)(2,1)} %collective-permute-done.2), channel_id=1, source_target_pairs={{0,16},{16,32},{32,48},{48,64},{64,80},{80,96},{96,112},{112,128},... | collective-permute-start | bytes 6291464 | tf_op jit(solution)/shard_map/ppermute | solution.py:12
  206.5 2.2 copy-start.8
  206.5 2.8 copy-start.6
  208.7 1.7 copy-start.2
  212.8 258.6 %reduce-scatter.2.cloned.1.call-start = ((), (), s32[]{:S(2)}) async-start(), calls=%async_computation.2 | async-start | bytes 2228224 | tf_op jit(solution)/shard_map/reduce_scatter | solution.py:82
  351.6 49.6 %copy-start.1 = (f32[2048,2,128]{2,0,1:T(8,128)S(1)}, f32[2048,2,128]{2,0,1:T(8,128)}, u32[]{:S(2)}) copy-start(f32[2048,2,128]{2,0,1:T(8,128)} %all-reduce.2.cloned.1.call-done) | copy-start | bytes 6291460
  401.1 2.0 copy-start.3
  403.1 2.0 copy-start.4
  403.1 2.3 copy-start.7
  404.3 2.2 copy-start.9
Sparse Core Ops, SparseCore 0:
  212.9 138.6 all-reduce.1
  409.1 62.2 reduce-scatter.1
where the time goes:
time: 480 us
  waiting for transfers between devices  374 us (78%)
  other arithmetic  47.7 us (10%)
  matrix products  19.8 us (4%)
  between operations  15.7 us (3%)
  starting transfers between devices  15.4 us (3%)
  local copies, waits for them, and re-layouts  7.61 us (2%)
    ppermute x4, waiting for transfers between devices, passed_along(): lax.ppermute(x, axis, [(i, (i + by) % length) for i in range(length)])  174 us
    psum x1, waiting for transfers between devices, on_device(): total_sketch = lax.psum(local_sketch, 'layer')  139 us
    reduce_scatter x1, waiting for transfers between devices, on_device(): lax.psum_scatter(jnp.stack(term_list, axis=1) / tile_size, 'layer', scatt...  60.7 us
    another operation x4, other arithmetic, orthonormal(): factor = jnp.linalg.cholesky(gram_mat)  23.6 us
    another operation x3, other arithmetic, orthonormal(): lax.linalg.triangular_solve(factor, by_cols, left_side=True, lower=True)  20 us
    ppermute x4, starting transfers between devices, passed_along(): lax.ppermute(x, axis, [(i, (i + by) % length) for i in range(length)])  15.1 us
  transfers between devices with their start and end apart: 6, of which 6 were waited for; matrix products, arithmetic and copies ran while one was open for 0% of the time, Pallas kernels for 0%

commit v1 on v0

--- a/solution.py
+++ b/solution.py
@@ -64,7 +64,11 @@
         partners.append(partner[0].astype(jnp.float32))
     mixed = jnp.stack(mixers, axis=1)
     local_sketch = jnp.einsum("kbr,ksrq->bsq", left_full, mixed, precision=high)
-    total_sketch = lax.psum(local_sketch, "layer")
+    total_sketch = local_sketch
+    for hop in (1, 2, 4, 8):
+        total_sketch = total_sketch + lax.ppermute(
+            total_sketch, "layer", [(dev, dev ^ hop) for dev in range(16)]
+        )
     basis_all = orthonormal(total_sketch, gram_of(total_sketch, tile_size))
     first_own = lax.axis_index("layer") * share_rows
     basis_part = lax.dynamic_slice_in_dim(basis_all, first_own, share_rows, 0)

time: 480 us -> 606 us (1.26)
  the two profiles are of different devices: /device:TPU:2 before, /device:TPU:4 now
where the time goes in v1:
time: 606 us
  waiting for transfers between devices  473 us (78%)
  other arithmetic  48.4 us (8%)
  starting transfers between devices  41.8 us (7%)
  matrix products  17.9 us (3%)
  between operations  15.7 us (3%)
  local copies, waits for them, and re-layouts  8.6 us (1%)
    ppermute x4, waiting for transfers between devices, on_device(): lax.ppermute(total_sketch, 'layer', [(dev, dev ^ hop) for dev in range(16)])  231 us
    ppermute x4, waiting for transfers between devices, passed_along(): lax.ppermute(x, axis, [(i, (i + by) % length) for i in range(length)])  175 us
    reduce_scatter x1, waiting for transfers between devices, on_device(): lax.psum_scatter(jnp.stack(term_list, axis=1) / tile_size, 'layer', scatt...  67.5 us
    ppermute x4, starting transfers between devices, on_device(): lax.ppermute(total_sketch, 'layer', [(dev, dev ^ hop) for dev in range(16)])  25.1 us
    another operation x4, other arithmetic, orthonormal(): factor = jnp.linalg.cholesky(gram_mat)  23.6 us
    another operation x3, other arithmetic, orthonormal(): lax.linalg.triangular_solve(factor, by_cols, left_side=True, lower=True)  20 us
    ppermute x4, starting transfers between devices, passed_along(): lax.ppermute(x, axis, [(i, (i + by) % length) for i in range(length)])  16.6 us
  transfers between devices with their start and end apart: 9, of which 9 were waited for; matrix products, arithmetic and copies ran while one was open for 0% of the time, Pallas kernels for 0%

profile of v1, /device:TPU:4, one launch (start us, length us, event | category | flops | bytes accessed | tf_op | source)
XLA Modules:
  0.0 605.8 jit_solution(15716613199220405674)
XLA Ops:
  7.2 0.8 compare_convert_fusion
  8.0 1.7 broadcast_multiply_fusion.1
  9.9 3.1 collective-permute-start
  13.0 46.1 %collective-permute-done = bf16[2,2,2048,128]{3,2,1,0:T(8,128)(2,1)S(1)} collective-permute-done((bf16[2,2,2048,128]{3,2,1,0:T(8,128)(2,1)S(1)}, bf16[2,2,2048,128]{3,2,1,0:T(8,128)(2,1)S(1)}, u32[]{:S(2)}, u32[]{:S(2)}) %collective-permute-start) | collective-permute-done | bytes 2097184 | tf_op jit(solution)/shard_map/ppermute | solution.py:12
  59.2 3.1 collective-permute-start.1
  62.3 45.3 %collective-permute-done.1 = bf16[2,2,2048,128]{3,2,1,0:T(8,128)(2,1)S(1)} collective-permute-done((bf16[2,2,2048,128]{3,2,1,0:T(8,128)(2,1)S(1)}, bf16[2,2,2048,128]{3,2,1,0:T(8,128)(2,1)S(1)}, u32[]{:S(2)}, u32[]{:S(2)}) %collective-permute-start.1) | collective-permute-done | bytes 2097184 | tf_op jit(solution)/shard_map/ppermute | solution.py:12
  107.5 4.2 collective-permute-start.2
  111.8 43.3 %collective-permute-done.2 = bf16[2,2,2048,128]{3,2,1,0:T(8,128)(2,1)} collective-permute-done((bf16[2,2,2048,128]{3,2,1,0:T(8,128)(2,1)S(1)}, bf16[2,2,2048,128]{3,2,1,0:T(8,128)(2,1)}, u32[]{:S(2)}, u32[]{:S(2)}) %collective-permute-start.2) | collective-permute-done | bytes 2097184 | tf_op jit(solution)/shard_map/ppermute | solution.py:12
  155.1 6.2 %collective-permute-start.3 = (bf16[2,2,2048,128]{3,2,1,0:T(8,128)(2,1)}, bf16[2,2,2048,128]{3,2,1,0:T(8,128)(2,1)}, u32[]{:S(2)}, u32[]{:S(2)}) collective-permute-start(bf16[2,2,2048,128]{3,2,1,0:T(8,128)(2,1)} %collective-permute-done.2), channel_id=1, source_target_pairs={{0,16},{16,32},{32,48},{48,64},{64,80},{80,96},{96,112},{112,128},... | collective-permute-start | bytes 6291464 | tf_op jit(solution)/shard_map/ppermute | solution.py:12
  161.3 0.6 fusion.30
  163.2 40.6 %collective-permute-done.3 = bf16[2,2,2048,128]{3,2,1,0:T(8,128)(2,1)} collective-permute-done((bf16[2,2,2048,128]{3,2,1,0:T(8,128)(2,1)}, bf16[2,2,2048,128]{3,2,1,0:T(8,128)(2,1)}, u32[]{:S(2)}, u32[]{:S(2)}) %collective-permute-start.3) | collective-permute-done | bytes 2097184 | tf_op jit(solution)/shard_map/ppermute | solution.py:12
  203.8 1.4 conditional.2
  203.8 1.4 copy.34
  205.2 2.0 fusion.8
  207.2 1.4 conditional.3
  207.2 1.4 copy.31
  208.6 2.2 fusion.7
  210.8 0.5 fusion.11
  211.4 0.5 fusion.12
  211.9 0.3 convolution_bitcast_fusion.4
  212.2 0.3 convolution_bitcast_fusion.3
  212.5 1.0 convolution_bitcast_fusion
  213.5 1.9 collective-permute-start.4
  215.4 4.1 collective-permute-done.4
  219.5 0.2 add.31
  219.8 8.5 %collective-permute-start.5 = (f32[2048,2,128]{2,0,1:T(8,128)S(1)}, f32[2048,2,128]{2,0,1:T(8,128)S(1)}, u32[]{:S(2)}, u32[]{:S(2)}) collective-permute-start(f32[2048,2,128]{2,0,1:T(8,128)S(1)} %add.31), channel_id=1, source_target_pairs={{0,2},{1,3},{2,0},{3,1},{4,6},{5,7},{6,4},{7,5},{8,10},{9,11},{10,... | collective-permute-start | bytes 6291464 | tf_op jit(solution)/shard_map/ppermute | solution.py:69
  228.3 45.9 %collective-permute-done.5 = f32[2048,2,128]{2,0,1:T(8,128)S(1)} collective-permute-done((f32[2048,2,128]{2,0,1:T(8,128)S(1)}, f32[2048,2,128]{2,0,1:T(8,128)S(1)}, u32[]{:S(2)}, u32[]{:S(2)}) %collective-permute-start.5) | collective-permute-done | bytes 2097184 | tf_op jit(solution)/shard_map/ppermute | solution.py:69
  274.2 0.2 add.32
  274.4 6.1 %collective-permute-start.6 = (f32[2048,2,128]{2,0,1:T(8,128)S(1)}, f32[2048,2,128]{2,0,1:T(8,128)S(1)}, u32[]{:S(2)}, u32[]{:S(2)}) collective-permute-start(f32[2048,2,128]{2,0,1:T(8,128)S(1)} %add.32), channel_id=1, source_target_pairs={{0,4},{1,5},{2,6},{3,7},{4,0},{5,1},{6,2},{7,3},{8,12},{9,13},{10,... | collective-permute-start | bytes 6291464 | tf_op jit(solution)/shard_map/ppermute | solution.py:69
  280.5 90.3 %collective-permute-done.6 = f32[2048,2,128]{2,0,1:T(8,128)S(1)} collective-permute-done((f32[2048,2,128]{2,0,1:T(8,128)S(1)}, f32[2048,2,128]{2,0,1:T(8,128)S(1)}, u32[]{:S(2)}, u32[]{:S(2)}) %collective-permute-start.6) | collective-permute-done | bytes 2097184 | tf_op jit(solution)/shard_map/ppermute | solution.py:69
  371.1 8.6 %collective-permute-start.7 = (f32[2048,2,128]{2,0,1:T(8,128)S(1)}, f32[2048,2,128]{2,0,1:T(8,128)S(1)}, u32[]{:S(2)}, u32[]{:S(2)}) collective-permute-start(f32[2048,2,128]{2,0,1:T(8,128)S(1)} %add.33), channel_id=1, source_target_pairs={{0,8},{1,9},{2,10},{3,11},{4,12},{5,13},{6,14},{7,15},{8,0},{9,1},... | collective-permute-start | bytes 6291464 | tf_op jit(solution)/shard_map/ppermute | solution.py:69
  379.7 90.1 %collective-permute-done.7 = f32[2048,2,128]{2,0,1:T(8,128)S(1)} collective-permute-done((f32[2048,2,128]{2,0,1:T(8,128)S(1)}, f32[2048,2,128]{2,0,1:T(8,128)S(1)}, u32[]{:S(2)}, u32[]{:S(2)}) %collective-permute-start.7) | collective-permute-done | bytes 2097184 | tf_op jit(solution)/shard_map/ppermute | solution.py:69
  469.9 1.3 copy-done.4
  471.2 3.6 fusion.14
  474.9 23.5 %custom-call.7 = f32[2,128,128]{2,1,0:T(8,128)S(1)} custom-call(f32[2,128,128]{2,1,0:T(8,128)S(1)} %fusion.28), custom_call_target="Cholesky" | custom-call | tf_op jit(solution)/shard_map/jit(cholesky)/cholesky | solution.py:20
  498.6 19.9 %custom-call.8 = f32[2,1,128,128]{2,3,1,0:T(8,128)S(1)} custom-call(f32[2,1,128,128]{3,2,1,0:T(8,128)S(1)} %select_bitcast_fusion), custom_call_target="InvertDiagBlocksLowerTriangular" | custom-call | tf_op jit(solution)/shard_map/triangular_solve | solution.py:22
  518.5 3.7 fusion.2
  522.2 1.2 fusion.4
  523.4 0.4 fusion.25
  523.8 0.4 fusion.26
  524.3 0.3 copy-done.7
  524.6 1.0 convolution_bitcast_fusion.1
  525.6 1.0 convolution_bitcast_fusion.2
  526.6 1.5 maximum_multiply_fusion
  528.1 0.9 dynamic-slice_bitcast_fusion
  529.0 0.8 copy.21
  529.8 67.5 %reduce-scatter.2.cloned.1.call-done = f32[128,2,128]{2,0,1:T(8,128)} async-done(((f32[2048,2,128]{2,0,1:T(8,128)}), f32[128,2,128]{2,0,1:T(8,128)}) %reduce-scatter.2.cloned.1.call-update) | async-done | bytes 131088 | tf_op jit(solution)/shard_map/reduce_scatter | solution.py:86
  597.3 1.7 copy.22
  (31 shorter events, 1.1 us)
Async XLA Ops:
  7.2 203.6 %copy-start = (bf16[2048,128]{1,0:T(8,128)(2,1)S(1)}, bf16[2048,128]{1,0:T(8,128)(2,1)}, u32[]{:S(2)}) copy-start(bf16[2048,128]{1,0:T(8,128)(2,1)} %param.15) | copy-start | bytes 1572868
  7.2 590.1 %reduce-scatter.2.cloned.1.call-start = ((), (), s32[]{:S(2)}) async-start(), calls=%async_computation.1 | async-start | bytes 2228224 | tf_op jit(solution)/shard_map/reduce_scatter | solution.py:86
  9.7 151.7 %copy-start.10 = (s32[1,2]{1,0:T(1,128)S(1)}, s32[1,2]{1,0:T(1,128)}, u32[]{:S(2)}) copy-start(s32[1,2]{1,0:T(1,128)} %param.17) | copy-start | bytes 28
  9.9 49.3 %collective-permute-start = (bf16[2,2,2048,128]{3,2,1,0:T(8,128)(2,1)S(1)}, bf16[2,2,2048,128]{3,2,1,0:T(8,128)(2,1)S(1)}, u32[]{:S(2)}, u32[]{:S(2)}) collective-permute-start(bf16[2,2,2048,128]{3,2,1,0:T(8,128)(2,1)S(1)} %pad_maximum_fusion), channel_id=1, source_target_pairs={{0,16},{16,32},{32,48},{48,64},{64,80},{80,96},{96,112},{112,128},... | collective-permute-start | bytes 6291464 | tf_op jit(solution)/shard_map/ppermute | solution.py:12
  59.2 144.6 %copy-start.5 = (bf16[2,2,2048,128]{3,2,1,0:T(8,128)(2,1)}, bf16[2,2,2048,128]{3,2,1,0:T(8,128)(2,1)S(1)}, u32[]{:S(2)}) copy-start(bf16[2,2,2048,128]{3,2,1,0:T(8,128)(2,1)S(1)} %collective-permute-done) | copy-start | bytes 6291460
  59.2 48.4 %collective-permute-start.1 = (bf16[2,2,2048,128]{3,2,1,0:T(8,128)(2,1)S(1)}, bf16[2,2,2048,128]{3,2,1,0:T(8,128)(2,1)S(1)}, u32[]{:S(2)}, u32[]{:S(2)}) collective-permute-start(bf16[2,2,2048,128]{3,2,1,0:T(8,128)(2,1)S(1)} %collective-permute-done), channel_id=1, source_target_pairs={{0,16},{16,32},{32,48},{48,64},{64,80},{80,96},{96,112},{112,128},... | collective-permute-start | bytes 6291464 | tf_op jit(solution)/shard_map/ppermute | solution.py:12
  107.5 47.6 %collective-permute-start.2 = (bf16[2,2,2048,128]{3,2,1,0:T(8,128)(2,1)S(1)}, bf16[2,2,2048,128]{3,2,1,0:T(8,128)(2,1)}, u32[]{:S(2)}, u32[]{:S(2)}) collective-permute-start(bf16[2,2,2048,128]{3,2,1,0:T(8,128)(2,1)S(1)} %collective-permute-done.1), channel_id=1, source_target_pairs={{0,16},{16,32},{32,48},{48,64},{64,80},{80,96},{96,112},{112,128},... | collective-permute-start | bytes 6291464 | tf_op jit(solution)/shard_map/ppermute | solution.py:12
  155.1 48.7 %collective-permute-start.3 = (bf16[2,2,2048,128]{3,2,1,0:T(8,128)(2,1)}, bf16[2,2,2048,128]{3,2,1,0:T(8,128)(2,1)}, u32[]{:S(2)}, u32[]{:S(2)}) collective-permute-start(bf16[2,2,2048,128]{3,2,1,0:T(8,128)(2,1)} %collective-permute-done.2), channel_id=1, source_target_pairs={{0,16},{16,32},{32,48},{48,64},{64,80},{80,96},{96,112},{112,128},... | collective-permute-start | bytes 6291464 | tf_op jit(solution)/shard_map/ppermute | solution.py:12
  208.6 2.2 copy-start.8
  208.6 2.9 copy-start.6
  210.8 1.7 copy-start.1
  213.5 6.1 collective-permute-start.4
  219.8 54.5 %collective-permute-start.5 = (f32[2048,2,128]{2,0,1:T(8,128)S(1)}, f32[2048,2,128]{2,0,1:T(8,128)S(1)}, u32[]{:S(2)}, u32[]{:S(2)}) collective-permute-start(f32[2048,2,128]{2,0,1:T(8,128)S(1)} %add.31), channel_id=1, source_target_pairs={{0,2},{1,3},{2,0},{3,1},{4,6},{5,7},{6,4},{7,5},{8,10},{9,11},{10,... | collective-permute-start | bytes 6291464 | tf_op jit(solution)/shard_map/ppermute | solution.py:69
  274.4 96.4 %collective-permute-start.6 = (f32[2048,2,128]{2,0,1:T(8,128)S(1)}, f32[2048,2,128]{2,0,1:T(8,128)S(1)}, u32[]{:S(2)}, u32[]{:S(2)}) collective-permute-start(f32[2048,2,128]{2,0,1:T(8,128)S(1)} %add.32), channel_id=1, source_target_pairs={{0,4},{1,5},{2,6},{3,7},{4,0},{5,1},{6,2},{7,3},{8,12},{9,13},{10,... | collective-permute-start | bytes 6291464 | tf_op jit(solution)/shard_map/ppermute | solution.py:69
  371.1 98.8 %collective-permute-start.7 = (f32[2048,2,128]{2,0,1:T(8,128)S(1)}, f32[2048,2,128]{2,0,1:T(8,128)S(1)}, u32[]{:S(2)}, u32[]{:S(2)}) collective-permute-start(f32[2048,2,128]{2,0,1:T(8,128)S(1)} %add.33), channel_id=1, source_target_pairs={{0,8},{1,9},{2,10},{3,11},{4,12},{5,13},{6,14},{7,15},{8,0},{9,1},... | collective-permute-start | bytes 6291464 | tf_op jit(solution)/shard_map/ppermute | solution.py:69
  469.9 1.3 copy-start.4
  518.5 3.7 copy-start.2
  522.2 2.0 copy-start.3
  522.2 2.3 copy-start.7
  523.4 2.2 copy-start.9
Sparse Core Ops, SparseCore 0:
  528.2 68.9 reduce-scatter.1
